TPU v7x, 512 devices: a whole 4x8x8 slice. The times are simulated.
512 devices in a mesh: elem: 16 (over x, z_hi), freq: 32 (over z_lo, y, core).
Axes of the slice: x: 4, y: 8, z: 8 (z_hi: 4, z_lo: 2; z = z_hi * 2 + z_lo), core: 2. Of those that a mesh axis runs over, the one named last changes fastest.
Arguments:
- pole_freq: float32 [16], replicated, may hold values from 0.05 to 0.95, as said below
- pole_damp: float32 [16], replicated, may hold values from 0.01 to 0.05
- samples: float32 [2, 32768, 6144], P(None, 'freq', 'elem'), may hold values from -30 to 30
Outputs:
- reduced: float32 [33, 33, 6144], P(None, None, ('elem', 'freq'))
- system: float32 [33, 33], replicated
- norm_row: float32 [33], replicated
Inputs may be any that keep to these rules, and one draw needn't show every extreme that they name: `pole_freq`: increasing; neighbours lie at least 0.54 / 16 apart.
All inputs are finite; a program needn't handle non-finite values.
Results may differ from a plain program's by a relative error of at most 0.0003.
Values sent between devices are 32-bit elements; how exact they have to be, the bound alone decides.
A program may use at most 64 MiB of HBM per device.

v0:
```python
import jax
import jax.numpy as jnp
from jax import lax
from jax.experimental import pallas as pl
from jax.experimental.pallas import tpu as pltpu
from jax.sharding import PartitionSpec as P

HIGH = lax.Precision.HIGHEST
MESH = pl.DeviceIdType.MESH
F32 = jnp.float32

NX, NZH, NZL, NY, NC = 4, 4, 2, 8, 2
NZ = NZH * NZL
NZY = NZL * NY
NFREQ = NZY * NC
QUAD = NZL * NC
PAIRS = 16
WIDTH = 2 * PAIRS + 1
ROWS = 40
BASIS = 48
OWN = 12
GROUP = 3
STRIDE = 40
TILES = OWN // GROUP
CHUNK = 256
CHUNKS = 4
LANES = 128
FREQ_LOCAL = 1024
ELEM_LOCAL = OWN * NFREQ
FREQ_TOTAL = FREQ_LOCAL * NFREQ
ELEM_TOTAL = ELEM_LOCAL * NX * NZH
INV_NF = 1.0 / FREQ_TOTAL


def iota(shape, dim):
    return lax.broadcasted_iota(jnp.int32, shape, dim)


def omega_of(half_position):
    return 0.02 + 0.98 * half_position / FREQ_TOTAL


def inverse_of(value):
    r = pltpu.reciprocal(value, approx=True)
    r = r * (2.0 - value * r)
    return r * (2.0 - value * r)


def split(value):
    high = value.astype(jnp.bfloat16)
    return high, (value - high.astype(F32)).astype(jnp.bfloat16)


def bf_dot(a, b):
    return jnp.dot(a, b, preferred_element_type=F32)


def wrap(value, size):
    return jnp.where(value >= size, value - size, value)


def tree_sum(values):
    values = list(values)
    while len(values) > 1:
        values = [a + b for a, b in zip(values[::2], values[1::2])] + values[len(values) & ~1 :]
    return values[0]


def pick(ref, index, shape):
    out = jnp.zeros(shape, F32)
    for m in range(PAIRS):
        out = jnp.where(index == m, ref[m], out)
    return out


def over_rows(col):
    return jnp.concatenate([col, col, jnp.zeros((8, LANES), F32)], axis=0)


def pair_coefs(ci, di, cj, dj, row_sum, col_sum):
    both = di + dj
    gap = cj - ci
    tot = ci + cj
    sq = both * both
    r1 = inverse_of(sq + gap * gap)
    r2 = inverse_of(sq + tot * tot)
    alpha, beta = both * r1, gap * r1
    gamma, delta = both * r2, -tot * r2
    ap, am = alpha + gamma, alpha - gamma
    bm, bp = beta - delta, beta + delta

    def table(di, bm, bp, row_sum, col_sum):
        ss, bd, bs, da = di * ap, di * bm, di * bp, di * am
        cr = jnp.where(row_sum, jnp.where(col_sum, ss, -bd), jnp.where(col_sum, bs, da))
        ce = jnp.where(row_sum, jnp.where(col_sum, bd, ss), jnp.where(col_sum, -da, bs))
        return cr, ce

    return table(di, bm, bp, row_sum, col_sum) + table(dj, -bp, -bm, col_sum, row_sum)


def coef_tables(c_col, d_col, pf, pd):
    shape = (ROWS, LANES)
    row, col = iota(shape, 0), iota(shape, 1)
    small = iota((8, LANES), 1) & (PAIRS - 1)
    cj, dj = pick(pf, small, (8, LANES)), pick(pd, small, (8, LANES))
    tall = lambda v: jnp.concatenate([v] * (ROWS // 8), axis=0)
    inside = (row < 2 * PAIRS) & (col < 2 * PAIRS)
    cr, ce, crt, cet = pair_coefs(
        over_rows(c_col), over_rows(d_col), tall(cj), tall(dj), row < PAIRS, col < PAIRS
    )
    last_row = row == 2 * PAIRS
    last_col = col == 2 * PAIRS
    one = lambda cond: jnp.where(cond, 1.0, 0.0).astype(F32)
    cr = jnp.where(inside, cr, one(last_row & ((col < PAIRS) | last_col)))
    ce = jnp.where(inside, ce, one(last_row & (col >= PAIRS) & (col < 2 * PAIRS)))
    crt = jnp.where(inside, crt, one(last_col & (row < PAIRS)))
    cet = jnp.where(inside, cet, one(last_col & (row >= PAIRS) & (row < 2 * PAIRS)))
    return cr, ce, crt, cet


def assemble(tables, r_row, e_row, r_col, e_col):
    cr, ce, crt, cet = tables
    return cr * r_row + ce * e_row + crt * over_rows(r_col) + cet * over_rows(e_col)


def row_to_col(row_vec, first):
    row, lane = iota((PAIRS, LANES), 0), iota((PAIRS, LANES), 1)
    kept = jnp.where(lane == row + first, jnp.broadcast_to(row_vec, (PAIRS, LANES)), 0.0)
    return jnp.broadcast_to(jnp.sum(kept, axis=1, keepdims=True), (PAIRS, LANES))


def rows_from(values):
    lane = iota(values.shape, 1)
    j = lane - jnp.where(lane >= 2 * STRIDE, 2 * STRIDE, jnp.where(lane >= STRIDE, STRIDE, 0))
    r_row = jnp.where(
        j < PAIRS,
        values,
        jnp.where(j < 2 * PAIRS, pltpu.roll(values, PAIRS, 1), jnp.where(j == 2 * PAIRS, values, 0.0)),
    )
    e_row = jnp.where(
        j < PAIRS,
        pltpu.roll(values, LANES - PAIRS, 1),
        jnp.where(j < 2 * PAIRS, values, 0.0),
    )
    return r_row, e_row


def eliminate(work):
    parts = [work[8 * b : 8 * b + 8] for b in range(ROWS // 8)]
    sub = iota((8, LANES), 0)
    for first in range(0, WIDTH, 8):
        count = min(8, WIDTH - first)
        b0 = first // 8
        live = range(b0, len(parts))
        cols = [
            [jnp.broadcast_to(parts[b][:, first + t : first + t + 1], (8, LANES)) for b in live]
            for t in range(count)
        ]
        rows = [parts[b0][t : t + 1, :] for t in range(count)]
        for t in range(count):
            inv = inverse_of(cols[t][0][t : t + 1, :])
            factor = [v * inv for v in cols[t]]
            factor[0] = jnp.where(sub > t, factor[0], 0.0)
            for u in range(t + 1, count):
                lead = cols[u][0][t : t + 1, :]
                cols[u] = [v - f * lead for v, f in zip(cols[u], factor)]
                rows[u] = rows[u] - factor[0][u : u + 1, :] * rows[t]
            for n, b in enumerate(live):
                parts[b] = parts[b] - factor[n] * rows[t]
    return jnp.concatenate(parts, axis=0)


def kernel(
    pf_hbm, pd_hbm, s_hbm, red_ref, sys_ref, nrm_ref,
    pf, pd, s_buf, re_buf, im_buf, xt_buf, pieces, recv_a, sum_a, recv_b,
    buf_m, buf_x, buf_y, buf_z,
    pole_sem, load_sem, send_sem, recv_sem,
):
    elem, freq = lax.axis_index("elem"), lax.axis_index("freq")
    x, z_hi = elem // NZH, elem % NZH
    zy, core = freq // NC, freq % NC
    z_lo, y = zy // NY, zy % NY
    z = z_hi * NZL + z_lo

    def at_freq(other):
        return {"elem": elem, "freq": other}

    def at_y(other):
        return {"elem": elem, "freq": (z_lo * NY + other) * NC + core}

    def far_first(size):
        return sorted(range(size), key=lambda d: -min(d, size - d))

    sibling = at_freq(zy * NC + (1 - core))
    zy_peers = [
        wrap(z_lo + dz, NZL) * NY + wrap(y + dy, NY)
        for dy in far_first(NY)
        for dz in (1, 0)
        if dy or dz
    ]
    y_peers = [at_y(wrap(y + dy, NY)) for dy in far_first(NY) if dy]
    z_peers = []
    for dz in far_first(NZ):
        if dz:
            to = wrap(z + dz, NZ)
            hi = to // NZL
            z_peers.append({"elem": x * NZH + hi, "freq": ((to - hi * NZL) * NY + y) * NC + core})
    x_peers = []
    for dx in far_first(NX):
        for c in (1, 0):
            if dx or c:
                to = wrap(x + dx, NX)
                x_peers.append({"elem": to * NZH + z_hi, "freq": zy * NC + wrap(core + c, NC)})
    corner = at_freq((wrap(z_lo + 1, NZL) * NY + y) * NC + (1 - core))

    pole_loads = [
        pltpu.make_async_copy(pf_hbm, pf, pole_sem.at[0]),
        pltpu.make_async_copy(pd_hbm, pd, pole_sem.at[1]),
    ]
    for load in pole_loads:
        load.start()
    loads = {}
    for k in range(CHUNKS):
        for part in range(2):
            at = pl.ds(k * CHUNK, CHUNK)
            loads[part, k] = pltpu.make_async_copy(
                s_hbm.at[part, at], s_buf.at[part, at], load_sem.at[part, k]
            )
            loads[part, k].start()

    barrier = pltpu.get_barrier_semaphore()

    def greet(device):
        pl.semaphore_signal(barrier, inc=1, device_id=device, device_id_type=MESH)

    z_rest = []
    for hi_step in range(1, NZH):
        hi = wrap(z_hi + hi_step, NZH)
        z_rest += [{"elem": x * NZH + hi, "freq": (lo * NY + y) * NC + core} for lo in range(NZL)]
    greets = [at_freq(zy_peer * NC + core) for zy_peer in zy_peers]
    greets += [corner] + z_rest + x_peers
    for device in greets:
        greet(device)
    greeted = len(greets)

    for load in pole_loads:
        load.wait()

    column = iota((PAIRS, LANES), 0)
    c_col = pick(pf, column, (PAIRS, LANES))
    d_col = pick(pd, column, (PAIRS, LANES))
    d_sq = d_col * d_col
    half16 = iota((PAIRS, LANES), 1).astype(F32) + 0.5
    base = (freq * FREQ_LOCAL).astype(F32)
    ones = jnp.where(iota((PAIRS, FREQ_LOCAL), 0) == 0, 1.0, 0.0)
    re_buf[2 * PAIRS : BASIS, :] = ones.astype(jnp.bfloat16)
    re_buf[BASIS + 2 * PAIRS :, :] = jnp.zeros((PAIRS, FREQ_LOCAL), jnp.bfloat16)
    for tile in range(FREQ_LOCAL // LANES):
        at = pl.ds(tile * LANES, LANES)
        w = omega_of(half16 + (base + tile * LANES))
        below, above = w - c_col, w + c_col
        i1 = inverse_of(d_sq + below * below)
        i2 = inverse_of(d_sq + above * above)
        first, second = below * i1, above * i2
        re_buf[0:PAIRS, at], re_buf[BASIS : BASIS + PAIRS, at] = split(d_sq * (i1 + i2))
        re_buf[PAIRS : 2 * PAIRS, at], re_buf[BASIS + PAIRS : BASIS + 2 * PAIRS, at] = split(
            d_col * (first - second)
        )
        im_buf[0:PAIRS, at], im_buf[2 * PAIRS : 3 * PAIRS, at] = split(-d_col * (first + second))
        im_buf[PAIRS : 2 * PAIRS, at], im_buf[3 * PAIRS :, at] = split(d_sq * (i1 - i2))

    quad = z_lo * NC + core
    share = NFREQ // QUAD
    halves = [slice(0, 8), slice(8, 16)]

    def mean_step(step, acc):
        acc = list(acc)
        start = ((quad * share + step) * FREQ_LOCAL).astype(F32)
        for tile in range(FREQ_LOCAL // LANES):
            w = omega_of(half16[0:8] + (start + tile * LANES))
            for h in range(2):
                below, above = w - c_col[halves[h]], w + c_col[halves[h]]
                n1 = d_sq[halves[h]] + below * below
                n2 = d_sq[halves[h]] + above * above
                r = inverse_of(n1 * n2)
                acc[2 * h] = acc[2 * h] + r * (n1 + n2)
                acc[2 * h + 1] = acc[2 * h + 1] + r * (below * n2 - above * n1)
        return tuple(acc)

    acc = lax.fori_loop(0, share, mean_step, (jnp.zeros((8, LANES), F32),) * 4)
    lane16 = iota((PAIRS, LANES), 1)
    sum_r = d_sq * jnp.sum(jnp.concatenate([acc[0], acc[2]], axis=0), axis=1, keepdims=True)
    sum_e = d_col * jnp.sum(jnp.concatenate([acc[1], acc[3]], axis=0), axis=1, keepdims=True)
    sums = jnp.where(lane16 == column, sum_r, jnp.where(lane16 == column + PAIRS, sum_e, 0.0))
    buf_m[quad] = jnp.sum(sums, axis=0, keepdims=True)

    x0 = jnp.zeros((BASIS, ELEM_LOCAL + LANES), F32)
    x1 = jnp.zeros((2 * PAIRS, ELEM_LOCAL), F32)
    for k in range(CHUNKS):
        at = pl.ds(k * CHUNK, CHUNK)
        loads[0, k].wait()
        loads[1, k].wait()
        s0, s1 = s_buf[0, at, :], s_buf[1, at, :]
        squares = s0 * s0 + s1 * s1
        power = tree_sum(squares[:, t * LANES : (t + 1) * LANES] for t in range(ELEM_LOCAL // LANES))
        high, low = split(jnp.concatenate([s0, power], axis=1))
        both = bf_dot(re_buf[:, at], high)
        x0 = x0 + (both[0:BASIS] + both[BASIS:] + bf_dot(re_buf[0:BASIS, at], low))
        high, low = split(s1)
        both = bf_dot(im_buf[:, at], high)
        x1 = x1 + (both[0 : 2 * PAIRS] + both[2 * PAIRS :] + bf_dot(im_buf[0 : 2 * PAIRS, at], low))
    x0, q = x0[:, 0:ELEM_LOCAL], x0[0:ROWS, ELEM_LOCAL:]

    stacked = jnp.concatenate(
        [
            x0,
            jnp.zeros((64 - BASIS, ELEM_LOCAL), F32),
            x1,
            jnp.zeros((LANES - 64 - 2 * PAIRS, ELEM_LOCAL), F32),
        ],
        axis=0,
    )
    for tile in range(ELEM_LOCAL // LANES):
        at = slice(tile * LANES, (tile + 1) * LANES)
        xt_buf[at, :] = stacked[:, at].T
    count = ELEM_LOCAL // GROUP
    thirds = [xt_buf[pl.ds(q, count, stride=GROUP), :] for q in range(GROUP)]
    lane_c = iota((count, LANES), 1)

    def spread(shift):
        rolled = [
            pltpu.roll(thirds[q], (STRIDE * q + shift) % LANES, 1) if (STRIDE * q + shift) % LANES else thirds[q]
            for q in range(GROUP)
        ]
        return jnp.where(
            lane_c < STRIDE, rolled[0], jnp.where(lane_c < 2 * STRIDE, rolled[1], rolled[2])
        )

    part0, part1 = spread(0), spread(64)
    upper = iota((8, LANES), 0) < 4
    for k in range(NZY):
        v0, v1 = part0[8 * k : 8 * k + 8], part1[8 * k : 8 * k + 8]
        pieces[0, k] = jnp.where(upper, v0, pltpu.roll(v1, 4, 0))
        pieces[1, k] = jnp.where(upper, pltpu.roll(v0, 4, 0), v1)

    pl.semaphore_wait(barrier, greeted)

    copy_a = pltpu.make_async_remote_copy(
        src_ref=pieces.at[1 - core],
        dst_ref=recv_a,
        send_sem=send_sem.at[5],
        recv_sem=recv_sem.at[5],
        device_id=sibling,
        device_id_type=MESH,
    )
    copy_a.start()
    for step in range(1, QUAD):
        lo, c = wrap(z_lo + step // NC, NZL), wrap(core + step % NC, NC)
        pltpu.make_async_remote_copy(
            src_ref=buf_m.at[quad],
            dst_ref=buf_m.at[quad],
            send_sem=send_sem.at[4],
            recv_sem=recv_sem.at[4],
            device_id=at_freq((lo * NY + y) * NC + c),
            device_id_type=MESH,
        ).start()

    tables = coef_tables(c_col, d_col, pf, pd)
    copy_a.wait_recv()
    for k in range(NZY):
        sum_a[k] = pieces[core, k] + recv_a[k]
    for other in zy_peers:
        pltpu.make_async_remote_copy(
            src_ref=sum_a.at[other],
            dst_ref=recv_b.at[zy],
            send_sem=send_sem.at[0],
            recv_sem=recv_sem.at[0],
            device_id=at_freq(other * NC + core),
            device_id_type=MESH,
        ).start()
    recv_b[zy] = sum_a[zy]

    rest = buf_m.at[pl.ds(0, QUAD - 1)]
    pltpu.make_async_copy(rest, rest, recv_sem.at[4]).wait()
    mean = tree_sum(buf_m[k] for k in range(QUAD)) * INV_NF
    lane1 = iota((1, LANES), 1)
    mean = jnp.where(lane1 == 2 * PAIRS, 1.0, mean)
    r_row, e_row = rows_from(mean)
    gram = assemble(tables, r_row, e_row, row_to_col(mean, 0), row_to_col(mean, PAIRS))
    row, lane = iota((ROWS, LANES), 0), iota((ROWS, LANES), 1)
    work = gram + jnp.where((lane == row + 64) & (row < WIDTH), 1.0, 0.0)
    work = eliminate(work)
    pivots = jnp.sum(jnp.where((lane == row) & (row < WIDTH), work, 0.0), axis=1, keepdims=True)
    pivots = jnp.where(iota((ROWS, 1), 0) < WIDTH, pivots, 1.0)
    inverse = pltpu.roll(work, 64, 1) * (1.0 / jnp.sqrt(pivots))
    inverse = jnp.where(lane < WIDTH, inverse, 0.0)

    q = jnp.broadcast_to(jnp.sum(q, axis=1, keepdims=True), (ROWS, LANES))
    q_row = jnp.sum(jnp.where(lane == row, q, 0.0), axis=0, keepdims=True)

    triple = [
        v + pltpu.roll(v, STRIDE, 1) + pltpu.roll(v, 2 * STRIDE, 1) for v in tables
    ]

    rest_b = recv_b.at[pl.ds(0, NZY - 1)]
    pltpu.make_async_copy(rest_b, rest_b, recv_sem.at[0]).wait()
    owned = tree_sum(recv_b[k] for k in range(NZY))
    owned = owned * (-INV_NF)

    other_part = pltpu.roll(owned, 4, 0)
    plus, minus = owned + other_part, owned - other_part
    r_rows, e_rows = rows_from(minus)
    plus_t = jnp.concatenate([plus, jnp.zeros((LANES - 8, LANES), F32)], axis=0).T
    lane16 = iota((PAIRS, LANES), 1)

    def columns(g, first):
        spread_col = [
            jnp.broadcast_to(
                plus_t[STRIDE * q + first : STRIDE * q + first + PAIRS, g : g + 1], (PAIRS, LANES)
            )
            for q in range(GROUP)
        ]
        return jnp.where(
            lane16 < STRIDE, spread_col[0], jnp.where(lane16 < 2 * STRIDE, spread_col[1], spread_col[2])
        )

    coupling = jnp.concatenate(
        [
            assemble(triple, r_rows[g : g + 1, :], e_rows[g : g + 1, :], columns(g, 0), columns(g, PAIRS))
            for g in range(TILES)
        ],
        axis=1,
    )
    reduced = jnp.dot(
        inverse[:, 0:ROWS], coupling, precision=HIGH, preferred_element_type=F32
    )
    parts = [reduced[:, g * LANES : (g + 1) * LANES] for g in range(TILES)]
    tall = jnp.concatenate(parts, axis=0)
    wide = jnp.dot(tall.T, tall, precision=HIGH, preferred_element_type=F32)
    corr = wide[0:ROWS]
    for q in range(1, GROUP):
        at = STRIDE * q
        corr = corr + pltpu.roll(wide[at : at + ROWS], LANES - at, 1)

    sub8, ln8 = iota((8, LANES), 0), iota((8, LANES), 1)
    spread8 = lambda v: jnp.broadcast_to(v, (8, LANES))
    border = jnp.where(
        sub8 == 0, spread8(corr[32:33]), jnp.where(sub8 == 1, spread8(q_row), 0.0)
    )
    packed = pltpu.roll(border, 80, 1)
    for g, first, shift in ((3, 80, 48), (2, 72, 40), (1, 56, 24)):
        packed = jnp.where(ln8 < first, pltpu.roll(corr[8 * g : 8 * g + 8], shift, 1), packed)
    total = jnp.where(ln8 < 32, corr[0:8], packed)

    def send(buf, me, peers, index, value):
        buf[me] = value
        for device in peers:
            pltpu.make_async_remote_copy(
                src_ref=buf.at[me],
                dst_ref=buf.at[me],
                send_sem=send_sem.at[index],
                recv_sem=recv_sem.at[index],
                device_id=device,
                device_id_type=MESH,
            ).start()

    def receive(buf, count, index):
        rest = buf.at[pl.ds(0, count - 1)]
        pltpu.make_async_copy(rest, rest, recv_sem.at[index]).wait()
        return tree_sum(buf[k] for k in range(count))

    send(buf_x, x * NC + core, x_peers, 1, total)

    for g in range(TILES):
        for q in range(GROUP):
            block = pltpu.roll(parts[g], LANES - STRIDE * q, 1) if q else parts[g]
            red_ref[GROUP * g + q] = block[0:WIDTH, 0:WIDTH]

    total = receive(buf_x, NX * NC, 1)
    send(buf_y, y, y_peers, 2, total)
    total = receive(buf_y, NY, 2)
    send(buf_z, z, z_peers, 3, total)
    total = receive(buf_z, NZ, 3)

    border = pltpu.roll(total, LANES - 80, 1)
    moments = jnp.where(lane1 < WIDTH, border[1:2], 0.0) * INV_NF
    mean_sq = moments[:, 2 * PAIRS : 2 * PAIRS + 1]
    r_row, e_row = rows_from(moments)
    data_gram = assemble(
        tables, r_row, e_row, row_to_col(moments, 0), row_to_col(moments, PAIRS)
    )
    half = jnp.concatenate(
        [total]
        + [pltpu.roll(total, LANES - shift, 1) for shift in (24, 40, 48)]
        + [spread8(border[0:1])],
        axis=0,
    )
    square = jnp.concatenate([half, jnp.zeros((LANES - ROWS, LANES), F32)], axis=0)
    stored = ((lane < 2 * PAIRS) & (lane >= (row & ~7))) | (row >= 2 * PAIRS)
    correction = jnp.where(stored, half, square.T[0:ROWS])
    system = (data_gram - correction) * (1.0 / mean_sq)
    sys_ref[...] = system[0:WIDTH, 0:WIDTH]
    nrm_ref[...] = (mean * jnp.sqrt(mean_sq * (1.0 / ELEM_TOTAL)))[:, 0:WIDTH]

    copy_a.wait_send()
    for buf, count, index in (
        (sum_a, NZY, 0), (buf_x, NX * NC, 1), (buf_y, NY, 2), (buf_z, NZ, 3), (buf_m, QUAD, 4)
    ):
        rest = buf.at[pl.ds(0, count - 1)]
        pltpu.make_async_copy(rest, rest, send_sem.at[index]).wait()


def writer(red, sys, nrm, red_out, sys_out, nrm_out):
    red_out[...] = red[...]
    sys_out[...] = sys[...]
    nrm_out[...] = nrm[...]


def per_device(pole_freq, pole_damp, samples):
    vmem = lambda *shape: pltpu.VMEM(shape, F32)
    in_hbm = lambda v: pltpu.with_memory_space_constraint(v, pltpu.HBM)
    half = lambda *shape: pltpu.VMEM(shape, jnp.bfloat16)
    results = (
        vmem(OWN, WIDTH, WIDTH),
        vmem(WIDTH, WIDTH),
        vmem(1, WIDTH),
    )
    reduced, system, norm_row = pl.pallas_call(
        kernel,
        out_shape=results,
        in_specs=[pl.BlockSpec(memory_space=pltpu.HBM)] * 3,
        out_specs=(pl.BlockSpec(memory_space=pltpu.VMEM),) * 3,
        scratch_shapes=[
            pltpu.SMEM((PAIRS,), F32),
            pltpu.SMEM((PAIRS,), F32),
            vmem(2, FREQ_LOCAL, ELEM_LOCAL),
            half(2 * BASIS, FREQ_LOCAL),
            half(4 * PAIRS, FREQ_LOCAL),
            vmem(ELEM_LOCAL, LANES),
            vmem(NC, NZY, 8, LANES),
            vmem(NZY, 8, LANES),
            vmem(NZY, 8, LANES),
            vmem(NZY, 8, LANES),
            vmem(QUAD, 1, LANES),
            vmem(NX * NC, 8, LANES),
            vmem(NY, 8, LANES),
            vmem(NZ, 8, LANES),
            pltpu.SemaphoreType.DMA((2,)),
            pltpu.SemaphoreType.DMA((2, CHUNKS)),
            pltpu.SemaphoreType.DMA((6,)),
            pltpu.SemaphoreType.DMA((6,)),
        ],
        compiler_params=pltpu.CompilerParams(
            collective_id=0, has_side_effects=True, vmem_limit_bytes=40 * 1024 * 1024
        ),
    )(*(in_hbm(v) for v in (pole_freq, pole_damp, samples)))
    in_vmem = lambda v: pltpu.with_memory_space_constraint(v, pltpu.VMEM)
    reduced, system, norm_row = pl.pallas_call(
        writer,
        out_shape=(
            jax.ShapeDtypeStruct((OWN, WIDTH, WIDTH), F32),
            jax.ShapeDtypeStruct((WIDTH, WIDTH), F32),
            jax.ShapeDtypeStruct((1, WIDTH), F32),
        ),
        in_specs=[pl.BlockSpec(memory_space=pltpu.VMEM)] * 3,
        out_specs=(pl.BlockSpec(memory_space=pltpu.VMEM),) * 3,
        compiler_params=pltpu.CompilerParams(vmem_limit_bytes=48 * 1024 * 1024),
    )(in_vmem(reduced), in_vmem(system), in_vmem(norm_row))
    return jnp.transpose(reduced, (1, 2, 0)), system, norm_row.reshape(WIDTH)


def solution(mesh):
    placed = (P(), P(), P(None, "freq", "elem"))
    return jax.shard_map(
        per_device,
        mesh=mesh,
        in_specs=placed,
        out_specs=(P(None, None, ("elem", "freq")), P(), P()),
        check_vma=False,
    )
```

profile of v0, /device:TPU:1, one launch (start us, length us, event | category | flops | bytes accessed | tf_op | source)
XLA Modules:
  0.0 34.5 jit_solution(15545053694338650535)
XLA Ops:
  0.6 33.1 %shard_map.58 = (f32[12,33,33]{2,1,0:T(8,128)S(1)}, f32[33,33]{1,0:T(8,128)S(1)}, f32[1,33]{1,0:T(1,128)S(1)}) custom-call(f32[16]{0:T(128)} %pf_hbm.1, f32[16]{0:T(128)} %pd_hbm.1, f32[2,1024,384]{2,1,0:T(8,128)} %s_hbm.1), custom_call_target="tpu_custom_call" | custom-call | tf_op jit(solution)/shard_map/pallas_call | solution.py:528
  33.8 0.7 %shard_map.59 = (f32[12,33,33]{2,1,0:T(8,128)}, f32[33,33]{1,0:T(8,128)}, f32[1,33]{1,0:T(1,128)}) custom-call(f32[12,33,33]{2,1,0:T(8,128)S(1)} %get-tuple-element.9.red, f32[33,33]{1,0:T(8,128)S(1)} %get-tuple-element.10.sys, f32[1,33]{1,0:T(1,128)S(1)} %get-tuple-element.11.nrm), custom_call_target="tpu_custom_call" | custom-call | tf_op jit(solution)/shard_map/pallas_call | solution.py:558
where the time goes:
time: 34.6 us; the launch traced here: 34.5 us
  Pallas kernels  33.8 us (98%)
  between operations  0.64 us (2%)
    pallas_call x1, Pallas kernels, per_device(): pl.pallas_call(kernel, out_shape=results, in_specs=[pl.BlockSpec(memory_s...  33.1 us
    pallas_call x1, Pallas kernels, per_device(): pl.pallas_call(writer, out_shape=(jax.ShapeDtypeStruct((OWN, WIDTH, WIDTH...  0.72 us

commit v1 on v0

--- a/solution.py
+++ b/solution.py
@@ -13,7 +13,6 @@
 NZ = NZH * NZL
 NZY = NZL * NY
 NFREQ = NZY * NC
-QUAD = NZL * NC
 PAIRS = 16
 WIDTH = 2 * PAIRS + 1
 ROWS = 40
@@ -173,7 +172,7 @@
 def kernel(
     pf_hbm, pd_hbm, s_hbm, red_ref, sys_ref, nrm_ref,
     pf, pd, s_buf, re_buf, im_buf, xt_buf, pieces, recv_a, sum_a, recv_b,
-    buf_m, buf_x, buf_y, buf_z,
+    buf_x, buf_y, buf_z,
     pole_sem, load_sem, send_sem, recv_sem,
 ):
     elem, freq = lax.axis_index("elem"), lax.axis_index("freq")
@@ -211,7 +210,6 @@
             if dx or c:
                 to = wrap(x + dx, NX)
                 x_peers.append({"elem": to * NZH + z_hi, "freq": zy * NC + wrap(core + c, NC)})
-    corner = at_freq((wrap(z_lo + 1, NZL) * NY + y) * NC + (1 - core))
 
     pole_loads = [
         pltpu.make_async_copy(pf_hbm, pf, pole_sem.at[0]),
@@ -219,14 +217,12 @@
     ]
     for load in pole_loads:
         load.start()
-    loads = {}
+    loads = []
     for k in range(CHUNKS):
-        for part in range(2):
-            at = pl.ds(k * CHUNK, CHUNK)
-            loads[part, k] = pltpu.make_async_copy(
-                s_hbm.at[part, at], s_buf.at[part, at], load_sem.at[part, k]
-            )
-            loads[part, k].start()
+        at = pl.ds(k * CHUNK, CHUNK)
+        load = pltpu.make_async_copy(s_hbm.at[:, at], s_buf.at[:, at], load_sem.at[k])
+        load.start()
+        loads.append(load)
 
     barrier = pltpu.get_barrier_semaphore()
 
@@ -238,7 +234,7 @@
         hi = wrap(z_hi + hi_step, NZH)
         z_rest += [{"elem": x * NZH + hi, "freq": (lo * NY + y) * NC + core} for lo in range(NZL)]
     greets = [at_freq(zy_peer * NC + core) for zy_peer in zy_peers]
-    greets += [corner] + z_rest + x_peers
+    greets += z_rest + x_peers
     for device in greets:
         greet(device)
     greeted = len(greets)
@@ -269,13 +265,12 @@
         im_buf[0:PAIRS, at], im_buf[2 * PAIRS : 3 * PAIRS, at] = split(-d_col * (first + second))
         im_buf[PAIRS : 2 * PAIRS, at], im_buf[3 * PAIRS :, at] = split(d_sq * (i1 - i2))
 
-    quad = z_lo * NC + core
-    share = NFREQ // QUAD
+    share = NFREQ // NC
     halves = [slice(0, 8), slice(8, 16)]
 
     def mean_step(step, acc):
         acc = list(acc)
-        start = ((quad * share + step) * FREQ_LOCAL).astype(F32)
+        start = ((core * share + step) * FREQ_LOCAL).astype(F32)
         for tile in range(FREQ_LOCAL // LANES):
             w = omega_of(half16[0:8] + (start + tile * LANES))
             for h in range(2):
@@ -292,14 +287,14 @@
     sum_r = d_sq * jnp.sum(jnp.concatenate([acc[0], acc[2]], axis=0), axis=1, keepdims=True)
     sum_e = d_col * jnp.sum(jnp.concatenate([acc[1], acc[3]], axis=0), axis=1, keepdims=True)
     sums = jnp.where(lane16 == column, sum_r, jnp.where(lane16 == column + PAIRS, sum_e, 0.0))
-    buf_m[quad] = jnp.sum(sums, axis=0, keepdims=True)
+    mean = jnp.sum(sums, axis=0, keepdims=True)
+    pieces[1 - core, NZY] = jnp.broadcast_to(mean, (8, LANES))
 
     x0 = jnp.zeros((BASIS, ELEM_LOCAL + LANES), F32)
     x1 = jnp.zeros((2 * PAIRS, ELEM_LOCAL), F32)
     for k in range(CHUNKS):
         at = pl.ds(k * CHUNK, CHUNK)
-        loads[0, k].wait()
-        loads[1, k].wait()
+        loads[k].wait()
         s0, s1 = s_buf[0, at, :], s_buf[1, at, :]
         squares = s0 * s0 + s1 * s1
         power = tree_sum(squares[:, t * LANES : (t + 1) * LANES] for t in range(ELEM_LOCAL // LANES))
@@ -348,23 +343,12 @@
     copy_a = pltpu.make_async_remote_copy(
         src_ref=pieces.at[1 - core],
         dst_ref=recv_a,
-        send_sem=send_sem.at[5],
-        recv_sem=recv_sem.at[5],
+        send_sem=send_sem.at[4],
+        recv_sem=recv_sem.at[4],
         device_id=sibling,
         device_id_type=MESH,
     )
     copy_a.start()
-    for step in range(1, QUAD):
-        lo, c = wrap(z_lo + step // NC, NZL), wrap(core + step % NC, NC)
-        pltpu.make_async_remote_copy(
-            src_ref=buf_m.at[quad],
-            dst_ref=buf_m.at[quad],
-            send_sem=send_sem.at[4],
-            recv_sem=recv_sem.at[4],
-            device_id=at_freq((lo * NY + y) * NC + c),
-            device_id_type=MESH,
-        ).start()
-
     tables = coef_tables(c_col, d_col, pf, pd)
     copy_a.wait_recv()
     for k in range(NZY):
@@ -380,9 +364,7 @@
         ).start()
     recv_b[zy] = sum_a[zy]
 
-    rest = buf_m.at[pl.ds(0, QUAD - 1)]
-    pltpu.make_async_copy(rest, rest, recv_sem.at[4]).wait()
-    mean = tree_sum(buf_m[k] for k in range(QUAD)) * INV_NF
+    mean = (mean + recv_a[NZY, 0:1, :]) * INV_NF
     lane1 = iota((1, LANES), 1)
     mean = jnp.where(lane1 == 2 * PAIRS, 1.0, mean)
     r_row, e_row = rows_from(mean)
@@ -410,7 +392,7 @@
     other_part = pltpu.roll(owned, 4, 0)
     plus, minus = owned + other_part, owned - other_part
     r_rows, e_rows = rows_from(minus)
-    plus_t = jnp.concatenate([plus, jnp.zeros((LANES - 8, LANES), F32)], axis=0).T
+    plus_t = plus.T
     lane16 = iota((PAIRS, LANES), 1)
 
     def columns(g, first):
@@ -504,7 +486,7 @@
 
     copy_a.wait_send()
     for buf, count, index in (
-        (sum_a, NZY, 0), (buf_x, NX * NC, 1), (buf_y, NY, 2), (buf_z, NZ, 3), (buf_m, QUAD, 4)
+        (sum_a, NZY, 0), (buf_x, NX * NC, 1), (buf_y, NY, 2), (buf_z, NZ, 3)
     ):
         rest = buf.at[pl.ds(0, count - 1)]
         pltpu.make_async_copy(rest, rest, send_sem.at[index]).wait()
@@ -537,18 +519,17 @@
             half(2 * BASIS, FREQ_LOCAL),
             half(4 * PAIRS, FREQ_LOCAL),
             vmem(ELEM_LOCAL, LANES),
-            vmem(NC, NZY, 8, LANES),
+            vmem(NC, NZY + 1, 8, LANES),
+            vmem(NZY + 1, 8, LANES),
             vmem(NZY, 8, LANES),
             vmem(NZY, 8, LANES),
-            vmem(NZY, 8, LANES),
-            vmem(QUAD, 1, LANES),
             vmem(NX * NC, 8, LANES),
             vmem(NY, 8, LANES),
             vmem(NZ, 8, LANES),
             pltpu.SemaphoreType.DMA((2,)),
-            pltpu.SemaphoreType.DMA((2, CHUNKS)),
-            pltpu.SemaphoreType.DMA((6,)),
-            pltpu.SemaphoreType.DMA((6,)),
+            pltpu.SemaphoreType.DMA((CHUNKS,)),
+            pltpu.SemaphoreType.DMA((5,)),
+            pltpu.SemaphoreType.DMA((5,)),
         ],
         compiler_params=pltpu.CompilerParams(
             collective_id=0, has_side_effects=True, vmem_limit_bytes=40 * 1024 * 1024

time: 34.6 us -> 34.8 us (level)
  no operation moved by 1% of the time
where the time goes in v1:
time: 34.8 us; the launch traced here: 34.7 us
  Pallas kernels  34 us (98%)
  between operations  0.64 us (2%)
    pallas_call x1, Pallas kernels, per_device(): pl.pallas_call(kernel, out_shape=results, in_specs=[pl.BlockSpec(memory_s...  33.3 us
    pallas_call x1, Pallas kernels, per_device(): pl.pallas_call(writer, out_shape=(jax.ShapeDtypeStruct((OWN, WIDTH, WIDTH...  0.72 us

profile of v1, /device:TPU:1, one launch (start us, length us, event | category | flops | bytes accessed | tf_op | source)
XLA Modules:
  0.0 34.7 jit_solution(17717834322375947166)
XLA Ops:
  0.6 33.3 %shard_map.58 = (f32[12,33,33]{2,1,0:T(8,128)S(1)}, f32[33,33]{1,0:T(8,128)S(1)}, f32[1,33]{1,0:T(1,128)S(1)}) custom-call(f32[16]{0:T(128)} %pf_hbm.1, f32[16]{0:T(128)} %pd_hbm.1, f32[2,1024,384]{2,1,0:T(8,128)} %s_hbm.1), custom_call_target="tpu_custom_call" | custom-call | tf_op jit(solution)/shard_map/pallas_call | solution.py:510
  33.9 0.7 %shard_map.59 = (f32[12,33,33]{2,1,0:T(8,128)}, f32[33,33]{1,0:T(8,128)}, f32[1,33]{1,0:T(1,128)}) custom-call(f32[12,33,33]{2,1,0:T(8,128)S(1)} %get-tuple-element.9.red, f32[33,33]{1,0:T(8,128)S(1)} %get-tuple-element.10.sys, f32[1,33]{1,0:T(1,128)S(1)} %get-tuple-element.11.nrm), custom_call_target="tpu_custom_call" | custom-call | tf_op jit(solution)/shard_map/pallas_call | solution.py:539
